TPU v7x, 32 devices: a whole 2x2x4 slice. The times are simulated.
32 devices in a mesh: dp: 16 (over z, y, x), rep: 2 (over core).
Axes of the slice: x: 2, y: 2, z: 4, core: 2. Of those that a mesh axis runs over, the one named last changes fastest.
Arguments:
- tokens: bfloat16 [16384, 1024], P(('dp', 'rep')), may hold values from -6 to 6
- kept_patch: int32 [16384], P(('dp', 'rep')), may hold values from 0 to 195
- image_lengths: int32 [32, 16], P(('dp', 'rep')), may hold values from 0 to 64, as said below
- ground_distance: int32 [32, 16], P(('dp', 'rep')), may hold values from 1 to 30
- cotangent: bfloat16 [16384, 1024], P(('dp', 'rep')), may hold values from -6 to 6
- norm_one_gain: bfloat16 [1024], P('dp'), may hold values from 0.5 to 1.5
- norm_one_bias: bfloat16 [1024], P('dp'), may hold values from -1.5 to 1.5
- joint_weight: bfloat16 [1024, 3072], P('dp'), may hold values from -0.1875 to 0.1875
- joint_bias: bfloat16 [3072], P('dp'), may hold values from -1.5 to 1.5
- merge_weight: bfloat16 [1024, 1024], P('dp'), may hold values from -0.5 to 0.5
- merge_bias: bfloat16 [1024], P('dp'), may hold values from -1.5 to 1.5
- norm_two_gain: bfloat16 [1024], P('dp'), may hold values from 0.5 to 1.5
- norm_two_bias: bfloat16 [1024], P('dp'), may hold values from -1.5 to 1.5
- expand_weight: bfloat16 [1024, 4096], P('dp'), may hold values from -0.1875 to 0.1875
- expand_bias: bfloat16 [4096], P('dp'), may hold values from -1.5 to 1.5
- shrink_weight: bfloat16 [4096, 1024], P('dp'), may hold values from -0.125 to 0.125
- shrink_bias: bfloat16 [1024], P('dp'), may hold values from -1.5 to 1.5
Outputs:
- output: bfloat16 [16384, 1024], P(('dp', 'rep'))
- grad_tokens: float32 [16384, 1024], P(('dp', 'rep'))
- grad_norm_one_gain: float32 [1024], P('dp')
- grad_norm_one_bias: float32 [1024], P('dp')
- grad_joint_weight: float32 [1024, 3072], P('dp')
- grad_joint_bias: float32 [3072], P('dp')
- grad_merge_weight: float32 [1024, 1024], P('dp')
- grad_merge_bias: float32 [1024], P('dp')
- grad_norm_two_gain: float32 [1024], P('dp')
- grad_norm_two_bias: float32 [1024], P('dp')
- grad_expand_weight: float32 [1024, 4096], P('dp')
- grad_expand_bias: float32 [4096], P('dp')
- grad_shrink_weight: float32 [4096, 1024], P('dp')
- grad_shrink_bias: float32 [1024], P('dp')
Inputs may be any that keep to these rules, and one draw needn't show every extreme that they name: In each row of image_lengths the slots are filled in order until 512 rows or fewer are used, the last image may be cut, later slots are 0 and the remaining rows are padding; some device has no padding rows and some slot holds 64 patches.
All inputs are finite; a program needn't handle non-finite values.
Results may differ from a plain program's by a relative error of at most 0.014.
Values may be sent and summed in bfloat16 or wider, within the bound.
A program may use at most 192 MiB of HBM per device.

v0:
```python
import jax
import jax.numpy as jnp
from jax import lax
from jax.sharding import PartitionSpec as P

HD = 64


def packing(lengths, row_count):
    image_ends = jnp.cumsum(lengths)
    row_ids = jnp.arange(row_count, dtype=jnp.int32)
    segment = jnp.sum((image_ends[None, :] <= row_ids[:, None]).astype(jnp.int32), axis=1)
    live_rows = (row_ids < image_ends[-1]).astype(jnp.float32)
    return (segment, live_rows)


def row_distance(segment, distances):
    slots = jnp.arange(distances.shape[-1], dtype=jnp.int32)
    onehot = (segment[:, None] == slots[None, :]).astype(jnp.float32)
    return jnp.sum(onehot * distances[None, :].astype(jnp.float32), axis=1)


def positions(patch_index, ground_rows, model_width):
    quarter = model_width // 4
    frequency = 1.0 / 10000.0 ** (jnp.arange(quarter, dtype=jnp.float32) / quarter)
    factor = ground_rows / 10.0
    across_rows = ((patch_index // 14).astype(jnp.float32) * factor)[..., None] * frequency
    along_rows = ((patch_index % 14).astype(jnp.float32) * factor)[..., None] * frequency
    return jnp.concatenate(
        [jnp.sin(across_rows), jnp.cos(across_rows), jnp.sin(along_rows), jnp.cos(along_rows)],
        axis=-1,
    )


def norm_forward(hidden, scaling, offset):
    center = hidden - jnp.mean(hidden, axis=-1, keepdims=True)
    inverse = lax.rsqrt(jnp.mean(center * center, axis=-1, keepdims=True) + 1e-06)
    scaled = center * inverse
    return (scaled * scaling.astype(jnp.float32) + offset.astype(jnp.float32), scaled, inverse)


def norm_backward(incoming, scaled, inverse, scaling):
    grad_scaled = incoming * scaling.astype(jnp.float32)
    centered_grad = grad_scaled - jnp.mean(grad_scaled, axis=-1, keepdims=True)
    centered_grad = centered_grad - scaled * jnp.mean(grad_scaled * scaled, axis=-1, keepdims=True)
    return (centered_grad * inverse, jnp.sum(incoming * scaled, axis=0), jnp.sum(incoming, axis=0))


def gelu_slope(hidden_pre):
    normal_cdf = 0.5 * (1.0 + jax.scipy.special.erf(hidden_pre * 0.7071067811865476))
    density = jnp.exp(-0.5 * hidden_pre * hidden_pre) * 0.3989422804014327
    return normal_cdf + hidden_pre * density


def on_device(
    tokens,
    kept_patch,
    image_lengths,
    ground_distance,
    cotangent,
    norm_one_gain,
    norm_one_bias,
    joint_weight,
    joint_bias,
    merge_weight,
    merge_bias,
    norm_two_gain,
    norm_two_bias,
    expand_weight,
    expand_bias,
    shrink_weight,
    shrink_bias,
):
    full = (
        lax.all_gather(norm_one_gain, "dp", axis=0, tiled=True),
        lax.all_gather(norm_one_bias, "dp", axis=0, tiled=True),
        lax.all_gather(joint_weight, "dp", axis=0, tiled=True),
        lax.all_gather(joint_bias, "dp", axis=0, tiled=True),
        lax.all_gather(merge_weight, "dp", axis=0, tiled=True),
        lax.all_gather(merge_bias, "dp", axis=0, tiled=True),
        lax.all_gather(norm_two_gain, "dp", axis=0, tiled=True),
        lax.all_gather(norm_two_bias, "dp", axis=0, tiled=True),
        lax.all_gather(expand_weight, "dp", axis=0, tiled=True),
        lax.all_gather(expand_bias, "dp", axis=0, tiled=True),
        lax.all_gather(shrink_weight, "dp", axis=0, tiled=True),
        lax.all_gather(shrink_bias, "dp", axis=0, tiled=True),
    )
    row_count = tokens.shape[0]
    model_width = tokens.shape[1]
    head_count = model_width // HD
    segment, live_rows = packing(image_lengths[0], row_count)
    ground_rows = row_distance(segment, ground_distance[0])
    residual_in = tokens.astype(jnp.float32) + positions(kept_patch, ground_rows, model_width)
    first, scaled_one, inverse_one = norm_forward(residual_in, full[0], full[1])
    first_low = first.astype(jnp.bfloat16)
    projected = (
        jnp.dot(first_low, full[2], preferred_element_type=jnp.float32)
        + full[3].astype(jnp.float32)
    ).astype(jnp.bfloat16)
    queries = projected[:, :model_width].reshape(row_count, head_count, HD)
    key_rows = projected[:, model_width : 2 * model_width].reshape(row_count, head_count, HD)
    value_rows = projected[:, 2 * model_width :].reshape(row_count, head_count, HD)
    score_scale = HD ** (-0.5)

    def block_scores():
        raw_scores = (
            jnp.einsum("qhd,khd->hqk", queries, key_rows, preferred_element_type=jnp.float32)
            * score_scale
        )
        same_image = segment[:, None] == segment[None, :]
        return jnp.where(same_image[None], raw_scores, -1000000000.0)

    scores = block_scores()
    highest_score = jnp.max(scores, axis=-1, keepdims=True)
    exponent = jnp.exp(scores - highest_score)
    row_total = jnp.sum(exponent, axis=-1, keepdims=True)
    softmax_rows = exponent / row_total
    log_totals = highest_score + jnp.log(row_total)
    attended_parts = jnp.einsum(
        "hqk,khd->qhd",
        softmax_rows.astype(jnp.bfloat16),
        value_rows,
        preferred_element_type=jnp.float32,
    )
    attended = attended_parts.reshape(row_count, model_width).astype(jnp.bfloat16)
    branch = jnp.dot(attended, full[4], preferred_element_type=jnp.float32) + full[5].astype(
        jnp.float32
    )
    middle = residual_in + branch
    second, scaled_two, inverse_two = norm_forward(middle, full[6], full[7])
    second_low = second.astype(jnp.bfloat16)
    hidden_pre = jnp.dot(second_low, full[8], preferred_element_type=jnp.float32) + full[9].astype(
        jnp.float32
    )
    active_low = jax.nn.gelu(hidden_pre, approximate=False).astype(jnp.bfloat16)
    branch_mlp = jnp.dot(active_low, full[10], preferred_element_type=jnp.float32) + full[
        11
    ].astype(jnp.float32)
    output = ((middle + branch_mlp) * live_rows[:, None]).astype(jnp.bfloat16)
    again = (
        lax.all_gather(norm_one_gain, "dp", axis=0, tiled=True),
        lax.all_gather(norm_one_bias, "dp", axis=0, tiled=True),
        lax.all_gather(joint_weight, "dp", axis=0, tiled=True),
        lax.all_gather(joint_bias, "dp", axis=0, tiled=True),
        lax.all_gather(merge_weight, "dp", axis=0, tiled=True),
        lax.all_gather(merge_bias, "dp", axis=0, tiled=True),
        lax.all_gather(norm_two_gain, "dp", axis=0, tiled=True),
        lax.all_gather(norm_two_bias, "dp", axis=0, tiled=True),
        lax.all_gather(expand_weight, "dp", axis=0, tiled=True),
        lax.all_gather(expand_bias, "dp", axis=0, tiled=True),
        lax.all_gather(shrink_weight, "dp", axis=0, tiled=True),
        lax.all_gather(shrink_bias, "dp", axis=0, tiled=True),
    )
    incoming = cotangent.astype(jnp.float32) * live_rows[:, None]
    incoming_low = incoming.astype(jnp.bfloat16)
    grad_shrink = jnp.einsum(
        "tf,to->fo", active_low, incoming_low, preferred_element_type=jnp.float32
    )
    grad_shrink_offset = jnp.sum(incoming_low.astype(jnp.float32), axis=0)
    grad_active = jnp.einsum(
        "to,fo->tf", incoming_low, again[10], preferred_element_type=jnp.float32
    )
    grad_hidden = (grad_active * gelu_slope(hidden_pre)).astype(jnp.bfloat16)
    grad_expand = jnp.einsum(
        "td,tf->df", second_low, grad_hidden, preferred_element_type=jnp.float32
    )
    grad_expand_offset = jnp.sum(grad_hidden.astype(jnp.float32), axis=0)
    grad_second = jnp.einsum("tf,df->td", grad_hidden, again[8], preferred_element_type=jnp.float32)
    back_two, grad_gain_two, grad_bias_two = norm_backward(
        grad_second, scaled_two, inverse_two, again[6]
    )
    grad_middle = incoming + back_two
    middle_low = grad_middle.astype(jnp.bfloat16)
    grad_merge = jnp.einsum("ti,to->io", attended, middle_low, preferred_element_type=jnp.float32)
    grad_merge_offset = jnp.sum(middle_low.astype(jnp.float32), axis=0)
    grad_attended = jnp.einsum(
        "to,io->ti", middle_low, again[4], preferred_element_type=jnp.float32
    )
    grad_attended = grad_attended.astype(jnp.bfloat16).reshape(row_count, head_count, HD)
    softmax_rows = jnp.exp(block_scores() - log_totals)
    grad_softmax = jnp.einsum(
        "qhd,khd->hqk", grad_attended, value_rows, preferred_element_type=jnp.float32
    )
    row_delta = jnp.sum(softmax_rows * grad_softmax, axis=-1, keepdims=True)
    grad_scores = (softmax_rows * (grad_softmax - row_delta) * score_scale).astype(jnp.bfloat16)
    grad_query_parts = jnp.einsum(
        "hqk,khd->qhd", grad_scores, key_rows, preferred_element_type=jnp.float32
    )
    grad_keys = jnp.einsum("hqk,qhd->khd", grad_scores, queries, preferred_element_type=jnp.float32)
    grad_values = jnp.einsum(
        "hqk,qhd->khd",
        softmax_rows.astype(jnp.bfloat16),
        grad_attended,
        preferred_element_type=jnp.float32,
    )
    grad_joint = jnp.concatenate(
        [
            grad_query_parts.reshape(row_count, model_width),
            grad_keys.reshape(row_count, model_width),
            grad_values.reshape(row_count, model_width),
        ],
        axis=1,
    ).astype(jnp.bfloat16)
    grad_joint_matrix = jnp.einsum(
        "td,tj->dj", first_low, grad_joint, preferred_element_type=jnp.float32
    )
    grad_joint_offset = jnp.sum(grad_joint.astype(jnp.float32), axis=0)
    grad_first = jnp.einsum("tj,dj->td", grad_joint, again[2], preferred_element_type=jnp.float32)
    back_one, grad_gain_one, grad_bias_one = norm_backward(
        grad_first, scaled_one, inverse_one, again[0]
    )
    grad_tokens = grad_middle + back_one
    grads_full = (
        grad_gain_one,
        grad_bias_one,
        grad_joint_matrix,
        grad_joint_offset,
        grad_merge,
        grad_merge_offset,
        grad_gain_two,
        grad_bias_two,
        grad_expand,
        grad_expand_offset,
        grad_shrink,
        grad_shrink_offset,
    )
    shares = (
        lax.psum_scatter(grads_full[0], "dp", scatter_dimension=0, tiled=True),
        lax.psum_scatter(grads_full[1], "dp", scatter_dimension=0, tiled=True),
        lax.psum_scatter(grads_full[2], "dp", scatter_dimension=0, tiled=True),
        lax.psum_scatter(grads_full[3], "dp", scatter_dimension=0, tiled=True),
        lax.psum_scatter(grads_full[4], "dp", scatter_dimension=0, tiled=True),
        lax.psum_scatter(grads_full[5], "dp", scatter_dimension=0, tiled=True),
        lax.psum_scatter(grads_full[6], "dp", scatter_dimension=0, tiled=True),
        lax.psum_scatter(grads_full[7], "dp", scatter_dimension=0, tiled=True),
        lax.psum_scatter(grads_full[8], "dp", scatter_dimension=0, tiled=True),
        lax.psum_scatter(grads_full[9], "dp", scatter_dimension=0, tiled=True),
        lax.psum_scatter(grads_full[10], "dp", scatter_dimension=0, tiled=True),
        lax.psum_scatter(grads_full[11], "dp", scatter_dimension=0, tiled=True),
    )
    totals = (
        lax.psum(shares[0].astype(jnp.bfloat16), "rep").astype(jnp.float32),
        lax.psum(shares[1].astype(jnp.bfloat16), "rep").astype(jnp.float32),
        lax.psum(shares[2].astype(jnp.bfloat16), "rep").astype(jnp.float32),
        lax.psum(shares[3].astype(jnp.bfloat16), "rep").astype(jnp.float32),
        lax.psum(shares[4].astype(jnp.bfloat16), "rep").astype(jnp.float32),
        lax.psum(shares[5].astype(jnp.bfloat16), "rep").astype(jnp.float32),
        lax.psum(shares[6].astype(jnp.bfloat16), "rep").astype(jnp.float32),
        lax.psum(shares[7].astype(jnp.bfloat16), "rep").astype(jnp.float32),
        lax.psum(shares[8].astype(jnp.bfloat16), "rep").astype(jnp.float32),
        lax.psum(shares[9].astype(jnp.bfloat16), "rep").astype(jnp.float32),
        lax.psum(shares[10].astype(jnp.bfloat16), "rep").astype(jnp.float32),
        lax.psum(shares[11].astype(jnp.bfloat16), "rep").astype(jnp.float32),
    )
    return (
        output,
        grad_tokens,
        totals[0],
        totals[1],
        totals[2],
        totals[3],
        totals[4],
        totals[5],
        totals[6],
        totals[7],
        totals[8],
        totals[9],
        totals[10],
        totals[11],
    )


def solution(mesh):
    return jax.shard_map(
        on_device,
        mesh=mesh,
        in_specs=(
            P(("dp", "rep"), None),
            P(("dp", "rep")),
            P(("dp", "rep"), None),
            P(("dp", "rep"), None),
            P(("dp", "rep"), None),
            P("dp"),
            P("dp"),
            P("dp", None),
            P("dp"),
            P("dp", None),
            P("dp"),
            P("dp"),
            P("dp"),
            P("dp", None),
            P("dp"),
            P("dp", None),
            P("dp"),
        ),
        out_specs=(
            P(("dp", "rep"), None),
            P(("dp", "rep"), None),
            P("dp"),
            P("dp"),
            P("dp", None),
            P("dp"),
            P("dp", None),
            P("dp"),
            P("dp"),
            P("dp"),
            P("dp", None),
            P("dp"),
            P("dp", None),
            P("dp"),
        ),
        check_vma=False,
    )
```

profile of v0, /device:TPU:0, one launch (start us, length us, event | category | flops | bytes accessed | tf_op | source)
XLA Modules:
  0.0 1476.4 jit_solution(17900740844109685705)
XLA Ops:
  21.3 80.0 %all-reduce.16 = (bf16[3072]{0:T(1024)(128)(2,1)S(1)}, bf16[1024]{0:T(1024)(128)(2,1)S(1)}, bf16[1024]{0:T(1024)(128)(2,1)S(1)}, bf16[1024]{0:T(1024)(128)(2,1)S...) all-reduce(bf16[3072]{0:T(1024)(128)(2,1)S(1)} %dynamic-update-slic, ...), channel_id=1, replica_groups=mesh['dp'=16,'rep'=2] {'dp'}, use_global_device_ids=true, to_apply=%add.2 | all-reduce | flops 9216 | bytes 36864
  102.1 35.5 %all-gather = bf16[16,1,256]{2,1,0:T(2,128)(2,1)S(1)} all-gather(bf16[1,1,256]{2,1,0:T(2,128)(2,1)S(1)} %reshape.190), channel_id=1, replica_groups=mesh['dp'=16,'rep'=2] {'dp'}, dimensions={0}, use_global_device_ids=true | all-gather | bytes 8704 | tf_op jit(solution)/shard_map/all_gather | solution.py:84
  138.4 3.7 multiply_sine_fusion.1
  144.3 6.9 add_convert_fusion
  154.6 2.7 copy.64
  159.6 8.5 fusion.65
  168.0 8.4 fusion.4
  176.4 7.9 fusion.34
  184.4 2.9 fusion.66
  189.0 96.4 %all-gather.10.cloned.1.call-done = bf16[1024,4096]{1,0:T(8,128)(2,1)} async-done(((bf16[64,4096]{1,0:T(8,128)(2,1)}), bf16[1024,4096]{1,0:T(8,128)(2,1)}) %all-gather.10.cloned.1.call-update) | async-done | bytes 8388624 | tf_op jit(solution)/shard_map/all_gather | solution.py:83
  285.3 27.7 %fusion.8 = (bf16[512,4096]{1,0:T(8,128)(2,1)}, f32[512,4096]{1,0:T(8,128)}) fusion(f32[4096]{0:T(1024)S(1)} %bitcast.65, bf16[1024,4096]{1,0:T(8,128)(2,1)} %all-gather.10.cloned.1.call-done, f32[512,1024]{1,0:T(8,128)} %copy-done.1, f32[1024]{0:T(1024)S(1)} %convert_element_type.198, f32[1024]{0:T(1024)S(1)} %convert_element_type.197, ...), kind=kOutput, calls=%fused_computation.14 | convolution fusion | flops 4436000768 | bytes 23097344 | tf_op jit(solution)/shard_map/dot_general | solution.py:132
  313.0 86.0 %all-gather.12.cloned.1.call-done = bf16[4096,1024]{1,0:T(8,128)(2,1)} async-done(((bf16[256,1024]{1,0:T(8,128)(2,1)}), bf16[4096,1024]{1,0:T(8,128)(2,1)}) %all-gather.12.cloned.1.call-update) | async-done | bytes 8388624 | tf_op jit(solution)/shard_map/all_gather | solution.py:85
  399.0 12.5 convert_reduce_fusion
  411.5 7.1 multiply_reduce_fusion.1
  421.2 3.3 fusion.50
  424.5 4.5 convolution_convert_fusion
  430.7 9.3 fusion.67
  440.0 24.1 %fusion.35 = bf16[16,64,512]{2,1,0:T(8,128)(2,1)} fusion(bf16[512,16,64]{0,2,1:T(8,128)(2,1)} %bitcast.49, f32[16,512,512]{1,2,0:T(8,128)} %fusion.67, f32[16,512,512]{1,2,0:T(8,128)} %get-tuple-element.68, f32[16,512]{1,0:T(8,128)S(1)} %log_add_fusion), kind=kOutput, calls=%fused_computation.69 | convolution fusion | flops 566764032 | bytes 35684352 | tf_op jit(solution)/shard_map/hqk,khd->qhd/dot_general | solution.py:186
  464.1 24.3 %fusion.38 = bf16[16,64,512]{2,1,0:T(8,128)(2,1)} fusion(bf16[512,16,64]{0,2,1:T(8,128)(2,1)} %bitcast.51, f32[16,512,512]{1,2,0:T(8,128)} %fusion.67, f32[16,512,512]{1,2,0:T(8,128)} %get-tuple-element.68, f32[16,512]{1,0:T(8,128)S(1)} %log_add_fusion), kind=kOutput, calls=%fused_computation.70 | convolution fusion | flops 566764032 | bytes 35684352 | tf_op jit(solution)/shard_map/hqk,qhd->khd/dot_general | solution.py:189
  488.5 8.7 fusion.41
  498.2 9.7 fusion.58
  508.2 13.3 fusion.60
  522.7 10.7 fusion.55
  537.7 8.8 multiply_reduce_fusion.2
  546.5 77.2 %all-reduce.15 = (bf16[1024]{0:T(1024)(128)(2,1)S(1)}, bf16[1024]{0:T(1024)(128)(2,1)S(1)}, bf16[3072]{0:T(1024)(128)(2,1)S(1)}, bf16[1024]{0:T(1024)(128)(2,1)S...) all-reduce(f32[1024]{0:T(1024)S(1)} %get-tuple-element.16, ...), channel_id=2, replica_groups=mesh['dp'=16,'rep'=2] {'dp'}, use_global_device_ids=true, to_apply=%region_15.16.clone | all-reduce | flops 13312 | bytes 79872
  624.3 2.5 all-reduce.17
  631.0 4.3 multiply_add_fusion
  637.1 91.7 %reduce-scatter.5.cloned.1.call-done = f32[64,3072]{1,0:T(8,128)} async-done(((f32[1024,3072]{1,0:T(8,128)}), f32[64,3072]{1,0:T(8,128)}) %reduce-scatter.5.cloned.1.call-update) | async-done | bytes 786448 | tf_op jit(solution)/shard_map/reduce_scatter | solution.py:230
  730.6 346.5 %reduce-scatter.9.cloned.1.call-done = f32[64,4096]{1,0:T(8,128)} async-done(((f32[1024,4096]{1,0:T(8,128)}), f32[64,4096]{1,0:T(8,128)}) %reduce-scatter.9.cloned.1.call-update) | async-done | bytes 1048592 | tf_op jit(solution)/shard_map/reduce_scatter | solution.py:236
  1079.2 352.4 %reduce-scatter.11.cloned.1.call-done = f32[256,1024]{1,0:T(8,128)} async-done(((f32[4096,1024]{1,0:T(8,128)}), f32[256,1024]{1,0:T(8,128)}) %reduce-scatter.11.cloned.1.call-update) | async-done | bytes 1048592 | tf_op jit(solution)/shard_map/reduce_scatter | solution.py:238
  1433.7 10.2 multiply_convert_fusion.1
  1444.0 17.7 %all-reduce.21.cloned.1.call-done = (bf16[64,3072]{1,0:T(8,128)(2,1)}, bf16[64,1024]{1,0:T(8,128)(2,1)}, bf16[64,4096]{1,0:T(8,128)(2,1)}, bf16[256,1024]{1,0:T(8,128)(2,1)}) async-done(((bf16[64,3072]{1,0:T(8,128)(2,1)}, bf16[64,1024]{1,0:T(8,128)(2,1)}, bf16[64,4096]{1,0:T(8,128)(2,1)}, bf16[256,1024]{1,0:T(8,128)(2,1)}), (bf16[64,3072]{1,0:T(8,128)(2,1)}, bf16[64,1024]{1,0:T(8,128)(2,1)}, ...) | async-done | bytes 1572880 | tf_op jit(solution)/shard_map/psum | solution.py:244
  (141 shorter events, 53.1 us)
Async XLA Ops:
  7.2 137.1 %all-gather.6.cloned.1.call-start = ((), (), s32[]{:S(2)}) async-start(), calls=%async_computation.4 | async-start | bytes 6684672 | tf_op jit(solution)/shard_map/all_gather | solution.py:77
  7.9 176.4 %all-gather.8.cloned.1.call-start = ((), (), s32[]{:S(2)}) async-start(), calls=%async_computation.5 | async-start | bytes 2228224 | tf_op jit(solution)/shard_map/all_gather | solution.py:79
  8.7 276.7 %all-gather.10.cloned.1.call-start = ((), (), s32[]{:S(2)}) async-start(), calls=%async_computation.6 | async-start | bytes 8912896 | tf_op jit(solution)/shard_map/all_gather | solution.py:83
  9.4 389.6 %all-gather.12.cloned.1.call-start = ((), (), s32[]{:S(2)}) async-start(), calls=%async_computation.7 | async-start | bytes 8912896 | tf_op jit(solution)/shard_map/all_gather | solution.py:85
  10.0 625.3 %reduce-scatter.7.cloned.1.call-start = ((), (), s32[]{:S(2)}) async-start(), calls=%async_computation.9 | async-start | bytes 4456448 | tf_op jit(solution)/shard_map/reduce_scatter | solution.py:232
  101.3 49.9 %copy-start.14 = (f32[1024]{0:T(1024)}, f32[1024]{0:T(1024)S(1)}, u32[]{:S(2)}) copy-start(f32[1024]{0:T(1024)S(1)} %convert_element_type.187) | copy-start | bytes 12292
  101.3 49.9 %copy-start.18 = (f32[1024]{0:T(1024)}, f32[1024]{0:T(1024)S(1)}, u32[]{:S(2)}) copy-start(f32[1024]{0:T(1024)S(1)} %convert_element_type.188) | copy-start | bytes 12292
  143.6 7.5 copy-start.12
  144.0 7.2 copy-start.16
  154.6 13.4 copy-start.4
  168.0 8.4 copy-start.5
  187.3 1.3 copy-start.1
  399.0 12.5 copy-start.2
  399.0 12.5 copy-start.21
  411.5 7.2 copy-start.10
  419.8 1.3 copy-start
  424.4 304.3 %reduce-scatter.5.cloned.1.call-start = ((), (), s32[]{:S(2)}) async-start(), calls=%async_computation.8 | async-start | bytes 13369344 | tf_op jit(solution)/shard_map/reduce_scatter | solution.py:230
  488.4 9.7 copy-start.8
  488.4 9.7 copy-start.9
  488.4 9.7 copy-start.13
  488.4 9.7 copy-start.15
  488.5 9.7 copy-start.17
  488.5 9.7 copy-start.19
  497.2 1.0 copy-start.6
  507.9 569.2 %reduce-scatter.9.cloned.1.call-start = ((), (), s32[]{:S(2)}) async-start(), calls=%async_computation.10 | async-start | bytes 17825792 | tf_op jit(solution)/shard_map/reduce_scatter | solution.py:236
  521.5 1.2 copy-start.11
  521.5 910.1 %reduce-scatter.11.cloned.1.call-start = ((), (), s32[]{:S(2)}) async-start(), calls=%async_computation.11 | async-start | bytes 17825792 | tf_op jit(solution)/shard_map/reduce_scatter | solution.py:238
  533.4 2.1 copy-start.20
  533.4 2.1 copy-start.7
  533.4 928.2 %all-reduce.21.cloned.1.call-start = ((), (), s32[]{:S(2)}) async-start(), calls=%async_computation.12 | async-start | bytes 3145728 | tf_op jit(solution)/shard_map/psum | solution.py:244
  635.3 798.4 %copy-start.3 = (f32[512,1024]{1,0:T(8,128)S(1)}, f32[512,1024]{1,0:T(8,128)}, u32[]{:S(2)}) copy-start(f32[512,1024]{1,0:T(8,128)} %copy-done.1) | copy-start | bytes 6291460
Sparse Core Ops, SparseCore 0:
  10.8 97.9 all-gather.5
  111.6 59.4 all-gather.7
  173.8 111.4 all-gather.9
  287.9 111.0 all-gather.11
  424.6 93.2 reduce-scatter.6
  523.4 205.2 reduce-scatter.4
  731.1 345.9 reduce-scatter.8
  1079.5 352.0 reduce-scatter.10
  1435.5 26.1 all-reduce.20
where the time goes:
time: 1480 us
  waiting for transfers between devices  993 us (67%)
  matrix products  200 us (14%)
  blocking collectives  195 us (13%)
  other arithmetic  44.3 us (3%)
  local copies, waits for them, and re-layouts  24.5 us (2%)
  between operations  18 us (1%)
    reduce_scatter x1, waiting for transfers between devices, on_device(): lax.psum_scatter(grads_full[10], 'dp', scatter_dimension=0, tiled=True)  352 us
    reduce_scatter x1, waiting for transfers between devices, on_device(): lax.psum_scatter(grads_full[8], 'dp', scatter_dimension=0, tiled=True)  347 us
    unnamed x2, blocking collectives  157 us
    all_gather x1, waiting for transfers between devices, on_device(): lax.all_gather(expand_weight, 'dp', axis=0, tiled=True)  96.4 us
    reduce_scatter x1, waiting for transfers between devices, on_device(): lax.psum_scatter(grads_full[2], 'dp', scatter_dimension=0, tiled=True)  91.7 us
    all_gather x1, waiting for transfers between devices, on_device(): lax.all_gather(shrink_weight, 'dp', axis=0, tiled=True)  86 us
    all_gather x1, blocking collectives, on_device(): lax.all_gather(expand_bias, 'dp', axis=0, tiled=True)  35.5 us
  transfers between devices with their start and end apart: 9, of which 6 were waited for; matrix products, arithmetic and copies ran while one was open for 16% of the time, Pallas kernels for 0%

commit v1 on v0

--- a/solution.py
+++ b/solution.py
@@ -1,10 +1,20 @@
+import functools
+
 import jax
 import jax.numpy as jnp
 from jax import lax
+from jax.experimental import pallas as pl
+from jax.experimental.pallas import tpu as pltpu
 from jax.sharding import PartitionSpec as P
 
 HD = 64
-
+MESH = pl.DeviceIdType.MESH
+F32 = jnp.float32
+BF16 = jnp.bfloat16
+NEVER = -1000000000.0
+VMEM_BYTES = 127 * 2**19
+LAST = (((1,), (1,)), ((), ()))
+FIRST = (((0,), (0,)), ((), ()))
 
 def packing(lengths, row_count):
     image_ends = jnp.cumsum(lengths)
@@ -52,7 +62,7 @@
     return normal_cdf + hidden_pre * density
 
 
-def on_device(
+def general_layer(
     tokens,
     kept_patch,
     image_lengths,
@@ -270,44 +280,785 @@
     )
 
 
+def contract(a, b, dims):
+    return lax.dot_general(a, b, dims, preferred_element_type=F32)
+
+
+def matmul(a, b):
+    return jnp.dot(a, b, preferred_element_type=F32)
+
+
+def span(start, size):
+    return pl.ds(start if isinstance(start, int) else pl.multiple_of(start, size), size)
+
+
+def layer_kernel(dims, names, *args):
+    r = dict(zip(names, args, strict=True))
+    Z, Y, X = dims
+    h0, live, seg, vec, cot = (r[k] for k in ("h0", "live", "seg", "vec", "cot"))
+    N1, QKV, OA, H1, N2, G, DU, EB = (r[k] for k in ("N1", "QKV", "OA", "H1", "N2", "G", "DU", "EB"))
+    SEG, L, V, XS, XR, OUTB, DA, VG = (
+        r[k] for k in ("SEG", "L", "V", "XS", "XR", "OUTB", "DA", "VG")
+    )
+    R, D = h0.shape
+    half_heads = D // HD // 2
+    HW = half_heads * HD
+    FC = DU.shape[1]
+    me = lax.axis_index("dp")
+    c = lax.axis_index("rep")
+    o = 1 - c
+    x = lax.rem(me, X)
+    y = lax.rem(me // X, Y)
+    z = me // (X * Y)
+    OS = XS.at[:, 0:HW]
+    own = span(c * R, R)
+    sib = span(o * R, R)
+
+    def at(zz, yy, xx):
+        return (zz * (Y * X) + yy * X + xx, c)
+
+    def zplus(d):
+        return lax.rem(z + d, Z)
+
+    def zminus(d):
+        return lax.rem(z + Z - d, Z)
+
+    to_x, to_y, to_o = at(z, y, 1 - x), at(z, 1 - y, x), (me, o)
+    to_z = [None] + [at(zplus(d), y, x) for d in range(1, Z)]
+
+    def remote(src, dst, ssem, rsem, to):
+        return pltpu.make_async_remote_copy(
+            src_ref=src, dst_ref=dst, send_sem=ssem, recv_sem=rsem, device_id=to, device_id_type=MESH
+        )
+
+    barrier = pltpu.get_barrier_semaphore()
+    for to in to_z[1:] + [to_x, to_y, to_o]:
+        pl.semaphore_signal(barrier, inc=1, device_id=to, device_id_type=MESH)
+    pl.semaphore_wait(barrier, Z - 1 + 3)
+
+    pair_sems = iter(range(r["ps"].shape[0]))
+
+    def to_pair(src, dst):
+        k = next(pair_sems)
+        cp = remote(src, dst, r["ps"].at[k], r["pr"].at[k], to_o)
+        cp.start()
+        return cp
+
+    W = {k: r["W" + k] for k in "jmxs"}
+    rows = {k: W[k].shape[3] for k in W}
+    wid = {"j": W["j"].shape[4] // 2, "m": HW // 2, "x": W["x"].shape[4] // 2, "s": W["s"].shape[4] // 2}
+
+    def wcols(k, p):
+        if k == "m":
+            return span(c * HW + p * wid[k], wid[k])
+        return pl.ds(p * wid[k], wid[k])
+
+    def piece(k, p, zz, yy, xx):
+        return W[k].at[zz, yy, xx, :, wcols(k, p)]
+
+    order = "jmxs"
+    num = {(k, p): 2 * i + p for i, k in enumerate(order) for p in (0, 1)}
+
+    def send_piece(k, p, zz, yy, xx, ssem, rsem, to):
+        remote(piece(k, p, zz, yy, xx), piece(k, p, zz, yy, xx), ssem, rsem, to).start()
+
+    def vec_send(src, slot, to, sems):
+        cp = remote(src, r["VR"].at[slot], sems[0].at[slot], sems[1].at[slot], to)
+        cp.start()
+        return cp
+
+    vcps = [vec_send(vec, d - 1, to_z[d], (r["vs"], r["vr"])) for d in range(1, Z)]
+    segcp = to_pair(seg, SEG.at[c])
+    SEG[c] = seg[...]
+
+    lsem = r["ls"]
+    local = {k: [] for k in "jmxse"}
+
+    def local_copy(k, src, dst):
+        pltpu.make_async_copy(src, dst, lsem.at["jmxse".index(k)]).start()
+
+    for i in range(3):
+        local_copy("j", r["wj"].at[:, span(i * D + c * HW, HW)], W["j"].at[z, y, x, :, pl.ds(i * HW, HW)])
+    local_copy("m", r["wm"].at[:, span(c * HW, HW)], W["m"].at[z, y, x, :, span(c * HW, HW)])
+    blk = rows["s"]
+    for i in range(FC // blk):
+        local_copy("x", r["wx"].at[:, span(2 * blk * i + blk * c, blk)], W["x"].at[z, y, x, :, pl.ds(i * blk, blk)])
+    local_copy("s", r["ws"].at[span(c * blk, blk), :], W["s"].at[z, y, x])
+    local_copy("e", cot, EB.at[own, :])
+
+    def local_wait(k, ref):
+        pltpu.make_async_copy(ref, ref, lsem.at["jmxse".index(k)]).wait()
+
+    own_ref = {
+        "j": W["j"].at[z, y, x],
+        "m": W["m"].at[z, y, x, :, span(c * HW, HW)],
+        "x": W["x"].at[z, y, x],
+        "s": W["s"].at[z, y, x],
+    }
+    for k in order:
+        local_wait(k, own_ref[k])
+        for d in range(1, Z):
+            for p in (0, 1):
+                n = num[k, p]
+                send_piece(k, p, z, y, x, r["as1"].at[n], r["ar1"].at[n, d - 1], to_z[d])
+
+    def forward_z(k, d):
+        zs = zminus(d)
+        for p in (0, 1):
+            n = num[k, p]
+            if d:
+                cp = remote(piece(k, p, zs, y, x), piece(k, p, zs, y, x), r["as1"].at[n], r["ar1"].at[n, d - 1], to_z[d])
+                cp.wait_recv()
+            a, b = (to_y, to_x) if p == 0 else (to_x, to_y)
+            send_piece(k, p, zs, y, x, r["as2"].at[n], r["ar2"].at[n, d], a)
+            send_piece(k, p, zs, y, x, r["as3"].at[n], r["ar3"].at[n], b)
+
+    def forward_2(k, d):
+        zs = zminus(d)
+        for p in (0, 1):
+            n = num[k, p]
+            yy, xx, a, b = (1 - y, x, to_y, to_x) if p == 0 else (y, 1 - x, to_x, to_y)
+            remote(piece(k, p, zs, yy, xx), piece(k, p, zs, yy, xx), r["as2"].at[n], r["ar2"].at[n, d], a).wait_recv()
+            send_piece(k, p, zs, yy, xx, r["as3"].at[n], r["ar3"].at[n], b)
+
+    def gather_wait(k):
+        for p in (0, 1):
+            n = num[k, p]
+            ref = W[k].at[:, :, 0, :, wcols(k, p)] if p == 0 else W[k].at[:, 0, :, :, wcols(k, p)]
+            remote(ref, ref, r["as3"].at[n], r["ar3"].at[n], to_x if p == 0 else to_y).wait_recv()
+
+    def gather_done(k):
+        for p in (0, 1):
+            n = num[k, p]
+            for ref, s in (
+                (W[k].at[pl.ds(0, Z - 1), 0, 0, :, wcols(k, p)], "as1"),
+                (W[k].at[:, 0, 0, :, wcols(k, p)], "as2"),
+                (W[k].at[:, :, 0, :, wcols(k, p)], "as3"),
+            ):
+                remote(ref, ref, r[s].at[n], r["ar3"].at[n], to_x).wait_send()
+
+    events = []
+    for k in order:
+        events += [functools.partial(forward_z, k, d) for d in range(Z)]
+        events += [functools.partial(forward_2, k, d) for d in range(Z)]
+    events = events[::-1]
+
+    def pump(n):
+        for _ in range(n):
+            if events:
+                events.pop()()
+
+    per = 2 * Z
+
+    pump(1)
+    for d in range(1, Z):
+        vcps[d - 1].wait()
+    acc = vec[...].astype(F32)
+    for d in range(1, Z):
+        acc = acc + r["VR"][d - 1].astype(F32)
+    r["VT"][0] = acc.astype(BF16)
+    cp = vec_send(r["VT"].at[0], Z - 1, to_y, (r["vs"], r["vr"]))
+    cp.wait()
+    acc = acc + r["VR"][Z - 1].astype(F32)
+    r["VT"][1] = acc.astype(BF16)
+    cp = vec_send(r["VT"].at[1], Z, to_x, (r["vs"], r["vr"]))
+    cp.wait()
+    V[...] = acc + r["VR"][Z].astype(F32)
+    VG[...] = jnp.zeros_like(VG)
+
+    local_wait("e", EB.at[own, :])
+    def mask_rows(i, _):
+        rr = span(c * R + i * 128, 128)
+        EB[rr, :] = (EB[rr, :].astype(F32) * live[span(i * 128, 128), :]).astype(BF16)
+        VG[5:6, :] += jnp.sum(EB[rr, :].astype(F32), axis=0, keepdims=True)
+        return 0
+
+    lax.fori_loop(0, R // 128, mask_rows, 0)
+
+    def normed(h):
+        center = h - jnp.mean(h, axis=-1, keepdims=True)
+        inverse = lax.rsqrt(jnp.mean(center * center, axis=-1, keepdims=True) + 1e-06)
+        return center * inverse, inverse
+
+    def norm_one(i, _):
+        scaled, _i = normed(h0[span(i * 128, 128), :])
+        N1[span(c * R + i * 128, 128), :] = (scaled * V[0:1, :] + V[1:2, :]).astype(BF16)
+        return 0
+
+    lax.fori_loop(0, R // 128, norm_one, 0)
+    n1cp = to_pair(N1.at[own, :], N1.at[own, :])
+    ebcp = to_pair(EB.at[own, :], EB.at[own, :])
+    segcp.wait()
+    pump(per - 1)
+    n1cp.wait()
+    ebcp.wait()
+    pump(2)
+    gather_wait("j")
+
+    TQ = 256
+    for t in range(3 * HW // TQ):
+        w = W["j"][:, :, :, :, t * TQ : (t + 1) * TQ].reshape(D, TQ)
+        f = t * TQ
+        b = V[6 + f // D : 7 + f // D, f % D : f % D + TQ]
+        QKV[:, t * TQ : (t + 1) * TQ] = (matmul(N1[...], w) + b).astype(BF16)
+        pump(1)
+
+    lane = lax.broadcasted_iota(jnp.int32, (1, 2 * HD), 1) // HD
+
+    def same_image(g):
+        row = SEG[g, 0:1, :]
+        col = jnp.transpose(SEG[g])[:, 0:1]
+        return col == row
+
+    def attend(g, hp):
+        rr = span(g * R, R)
+        q = QKV[rr, span(hp * 2 * HD, 2 * HD)]
+        k = QKV[rr, span(HW + hp * 2 * HD, 2 * HD)]
+        v = QKV[rr, span(2 * HW + hp * 2 * HD, 2 * HD)]
+        same = same_image(g)
+        res = []
+        for i in (0, 1):
+            qi = jnp.where(lane == i, q.astype(F32) * HD**-0.5, 0.0).astype(BF16)
+            s = jnp.where(same, contract(k, qi, LAST), NEVER)
+            top = jnp.max(s, axis=0, keepdims=True)
+            e = jnp.exp(s - top)
+            tot = jnp.sum(e, axis=0, keepdims=True)
+            L[g * half_heads + 2 * hp + i] = top + jnp.log(tot)
+            pb = (e * (1.0 / tot)).astype(BF16)
+            res.append(contract(v, pb, FIRST)[i * HD : (i + 1) * HD])
+        return jnp.transpose(jnp.concatenate(res, axis=0)).astype(BF16)
+
+    for hp in range(half_heads // 2):
+        OS[:, 2 * HD * hp : 2 * HD * (hp + 1)] = attend(o, hp)
+        pump(1)
+    ocp = to_pair(OS, OA.at[:, span(c * HW, HW)])
+    for hp in range(half_heads // 2):
+        OA[:, span(c * HW + 2 * HD * hp, 2 * HD)] = attend(c, hp)
+        pump(1)
+    pump(max(0, len(events) - 2 * per + 2))
+    gather_wait("m")
+    wmcp = to_pair(W["m"].at[:, :, :, :, span(c * HW, HW)], W["m"].at[:, :, :, :, span(c * HW, HW)])
+    ocp.wait()
+    wmcp.wait()
+    pump(1)
+
+    TR = 256
+    for t in range(R // TR):
+        rr = pl.ds(t * TR, TR)
+        h1 = h0[rr, :] + matmul(OA[rr, :], W["m"][...].reshape(D, D)) + V[2:3, :]
+        H1[rr, :] = h1
+        scaled, _i = normed(h1)
+        N2[span(c * R + t * TR, TR), :] = (scaled * V[3:4, :] + V[4:5, :]).astype(BF16)
+    n2cp = to_pair(N2.at[own, :], N2.at[own, :])
+    pump(max(0, len(events) - per + 1))
+    n2cp.wait()
+    gather_wait("x")
+
+    for t in range(FC // TQ):
+        cc = slice(t * TQ, (t + 1) * TQ)
+        b = V[8 + t * TQ // D : 9 + t * TQ // D, t * TQ % D : t * TQ % D + TQ]
+        for h in range(2):
+            rr = slice(h * R, (h + 1) * R)
+            u = matmul(N2[rr, :], W["x"][:, :, :, :, cc].reshape(D, TQ)) + b
+            cdf = 0.5 * (1.0 + lax.erf(u * 0.7071067811865476))
+            G[rr, cc] = (u * cdf).astype(BF16)
+            DU[rr, cc] = (cdf + u * (jnp.exp(-0.5 * u * u) * 0.3989422804014327)).astype(BF16)
+        pump(1)
+
+    GS, GM, GX, GJ = r["GS"], r["GM"], W["s"], W["x"]
+    grad = {"s": GS, "x": GX, "m": GM, "j": GJ}
+    gorder = "sxmj"
+    gnum = {(k, p): 2 * i + p for i, k in enumerate(gorder) for p in (0, 1)}
+    R1, R2, R3 = ({k: r[n + k] for k in gorder} for n in ("R1", "R2", "R3"))
+    outs = {k: r["o" + k] for k in gorder}
+
+    def gslice(k, p):
+        if k == "s":
+            return slice(None), pl.ds(p * (D // 2), D // 2)
+        if k == "x":
+            return pl.ds(p * rows["x"], rows["x"]), slice(None)
+        if k == "m":
+            return slice(None), span(c * HW + p * (HW // 2), HW // 2)
+        return slice(None), pl.ds(p * (3 * HW // 2), 3 * HW // 2)
+
+    def add_into(ref, idx, other):
+        ref[idx] = (ref[idx].astype(F32) + other[...].astype(F32)).astype(BF16)
+
+    def rs_first(k, p):
+        n = gnum[k, p]
+        rs, cs = gslice(k, p)
+        if p == 0:
+            return remote(grad[k].at[:, :, 1 - x, rs, cs], R1[k].at[p], r["rs1"].at[n], r["rr1"].at[n], to_x)
+        return remote(grad[k].at[:, 1 - y, :, rs, cs], R1[k].at[p], r["rs1"].at[n], r["rr1"].at[n], to_y)
+
+    def rs_second(k, p):
+        n = gnum[k, p]
+        rs, cs = gslice(k, p)
+        if p == 0:
+            return remote(grad[k].at[:, 1 - y, x, rs, cs], R2[k].at[p], r["rs2"].at[n], r["rr2"].at[n], to_y)
+        return remote(grad[k].at[:, y, 1 - x, rs, cs], R2[k].at[p], r["rs2"].at[n], r["rr2"].at[n], to_x)
+
+    def rs_third(k, p, d):
+        n = gnum[k, p]
+        rs, cs = gslice(k, p)
+        return remote(grad[k].at[zplus(d), y, x, rs, cs], R3[k].at[p, d - 1], r["rs3"].at[n, d - 1], r["rr3"].at[n, d - 1], to_z[d])
+
+    def add_first(k, p):
+        rs_first(k, p).wait_recv()
+        rs, cs = gslice(k, p)
+        for q in (1, 0):
+            def one(i, _):
+                if p == 0:
+                    yy = y if q == 0 else 1 - y
+                    add_into(grad[k], (i, yy, x, rs, cs), R1[k].at[p, i, yy])
+                else:
+                    xx = x if q == 0 else 1 - x
+                    add_into(grad[k], (i, y, xx, rs, cs), R1[k].at[p, i, xx])
+                return 0
+
+            lax.fori_loop(0, Z, one, 0)
+            if q == 1:
+                rs_second(k, p).start()
+
+    def add_second(k, p):
+        rs_second(k, p).wait_recv()
+        rs, cs = gslice(k, p)
+
+        def one(i, _):
+            add_into(grad[k], (i, y, x, rs, cs), R2[k].at[p, i])
+            return 0
+
+        lax.fori_loop(0, Z, one, 0)
+        for d in range(1, Z):
+            rs_third(k, p, d).start()
+
+    def add_third(k, p):
+        for d in range(1, Z):
+            rs_third(k, p, d).wait_recv()
+        rs, cs = gslice(k, p)
+        tot = grad[k][z, y, x, rs, cs].astype(F32)
+        for d in range(1, Z):
+            tot = tot + R3[k][p, d - 1].astype(F32)
+        grad[k][z, y, x, rs, cs] = tot.astype(BF16)
+
+    fin_copies = []
+
+    def finish(k):
+        i = gorder.index(k)
+        cs = {"m": span(c * HW, HW), "j": pl.ds(0, 3 * HW)}.get(k, slice(None))
+        total = grad[k].at[z, y, x, :, cs]
+        a = pltpu.make_async_copy(total, outs[k].at[c], r["fl"].at[i])
+        b = remote(total, outs[k].at[c], r["fs"].at[i], r["fr"].at[i], to_o)
+        a.start()
+        b.start()
+        fin_copies.extend([a, b])
+
+    def first_pair(k):
+        for p in (0, 1):
+            rs_first(k, p).start()
+
+    def rs_events(k):
+        ev = [functools.partial(add_first, k, p) for p in (0, 1)]
+        ev += [functools.partial(add_second, k, p) for p in (0, 1)]
+        ev += [functools.partial(add_third, k, p) for p in (0, 1)]
+        return ev + [functools.partial(finish, k)]
+
+    FT = Y * X * rows["s"] // 2
+    nft = FC // FT
+    for t in range(nft):
+        g = contract(G[:, t * FT : (t + 1) * FT], EB[...], FIRST)
+        GS[t // 2, t % 2] = g.astype(BF16).reshape(X, rows["s"], D)
+        pump(1)
+    pump(len(events))
+    gather_wait("s")
+    first_pair("s")
+
+    for t in range(nft):
+        cc = slice(t * FT, (t + 1) * FT)
+        w = W["s"][t // 2, t % 2].reshape(FT, D)
+        vr = (8 + t * FT // D, t * FT % D)
+        for h in range(2):
+            rr = slice(h * R, (h + 1) * R)
+            du = (contract(EB[rr, :], w, LAST) * DU[rr, cc].astype(F32)).astype(BF16)
+            DU[rr, cc] = du
+            VG[vr[0] : vr[0] + 1, vr[1] : vr[1] + FT] += jnp.sum(du.astype(F32), axis=0, keepdims=True)
+
+    nt = D // TQ
+    for t in range(nt):
+        cc = slice(t * TQ, (t + 1) * TQ)
+        XS[:, cc] = matmul(G[sib, :], W["s"][:, :, :, :, cc].reshape(FC, TQ)).astype(BF16)
+    h2cp = to_pair(XS, OUTB)
+    events.extend(rs_events("s")[::-1])
+    h2cp.wait_recv()
+    for t in range(nt):
+        cc = slice(t * TQ, (t + 1) * TQ)
+        own_part = matmul(G[own, :], W["s"][:, :, :, :, cc].reshape(FC, TQ))
+        OUTB[:, cc] = ((H1[:, cc] + own_part + OUTB[:, cc].astype(F32) + V[5:6, cc]) * live[...]).astype(BF16)
+    outcp = pltpu.make_async_copy(OUTB, r["out"], r["fl"].at[len(gorder)])
+    outcp.start()
+    h2cp.wait_send()
+    gather_done("s")
+
+    def back_part(left, wk, n, rr_):
+        for t in range(Z):
+            w = wk[t][:, :, :, 0:n].reshape(Y * X * rows["j"], n)
+            cw = Y * X * rows["j"]
+            XS[:, t * cw : (t + 1) * cw] = contract(left[rr_, 0:n], w, LAST).astype(BF16)
+
+    back_part(DU, W["x"], FC, sib)
+    dn2cp = to_pair(XS, XR)
+
+    DT = Y * X * rows["x"]
+    for t in range(Z):
+        for p in (0, 1):
+            g = contract(N2[:, t * DT : (t + 1) * DT], DU[:, p * (FC // 2) : (p + 1) * (FC // 2)], FIRST)
+            GX[t, :, :, p * rows["x"] : (p + 1) * rows["x"], :] = g.astype(BF16).reshape(Y, X, rows["x"], FC // 2)
+    first_pair("x")
+    pump(2)
+    dn2cp.wait()
+
+    def norm_back(dy, scaled, inverse, gain, vg):
+        ds_ = dy * gain
+        VG[vg : vg + 1, :] += jnp.sum(dy * scaled, axis=0, keepdims=True)
+        VG[vg + 1 : vg + 2, :] += jnp.sum(dy, axis=0, keepdims=True)
+        cen = ds_ - jnp.mean(ds_, axis=-1, keepdims=True)
+        cen = cen - scaled * jnp.mean(ds_ * scaled, axis=-1, keepdims=True)
+        return cen * inverse
+
+    for t in range(R // TR):
+        rr = pl.ds(t * TR, TR)
+        dy = contract(DU[span(c * R + t * TR, TR), :], W["x"][...].reshape(D, FC), LAST) + XR[rr, :].astype(F32)
+        scaled, inverse = normed(H1[rr, :])
+        dh = EB[span(c * R + t * TR, TR), :].astype(F32) + norm_back(dy, scaled, inverse, V[3:4, :], 3)
+        H1[rr, :] = dh
+        DA[rr, :] = dh.astype(BF16)
+        VG[2:3, :] += jnp.sum(DA[rr, :].astype(F32), axis=0, keepdims=True)
+    gather_done("x")
+    pump(1)
+
+    for t in range(2):
+        base = o if t == 0 else c
+        for u in range(HW // (X * rows["m"])):
+            cw = X * rows["m"]
+            zz, yy = (base * (Z // 2) + u // Y), u % Y
+            w = W["m"][zz, yy].reshape(cw, D)
+            res = contract(DA[...], w, LAST).astype(BF16)
+            if t == 0:
+                OS[:, u * cw : (u + 1) * cw] = res
+            else:
+                G[own, 3 * HW + u * cw : 3 * HW + (u + 1) * cw] = res
+        if t == 0:
+            docp = to_pair(OS, G.at[own, pl.ds(3 * HW, HW)])
+    gather_done("m")
+    pump(1)
+
+    for t in range(Z):
+        g = contract(OA[:, t * DT : (t + 1) * DT], DA[...], FIRST)
+        GM[t] = g.astype(BF16).reshape(Y, X, rows["m"], D)
+    gmcp = to_pair(GM.at[:, :, :, :, span(o * HW, HW)], r["GMR"])
+
+    def attend_back(g, hp):
+        rr = span(g * R, R)
+        qc, kc, vc = (pl.ds(i * HW + hp * 2 * HD, 2 * HD) for i in range(3))
+        q, k, v = QKV[rr, qc], QKV[rr, kc], QKV[rr, vc]
+        do = G[rr, 3 * HW + hp * 2 * HD : 3 * HW + (hp + 1) * 2 * HD]
+        same = same_image(g)
+        dq, dk, dv = [], [], []
+        for i in (0, 1):
+            qi = jnp.where(lane == i, q.astype(F32) * HD**-0.5, 0.0).astype(BF16)
+            di = jnp.where(lane == i, do.astype(F32), 0.0).astype(BF16)
+            s = jnp.where(same, contract(k, qi, LAST), NEVER)
+            pr = jnp.exp(s - L[g * half_heads + 2 * hp + i])
+            dp = contract(v, di, LAST)
+            delta = jnp.sum(pr * dp, axis=0, keepdims=True)
+            dsb = (pr * (dp - delta) * HD**-0.5).astype(BF16)
+            dq.append(contract(k, dsb, FIRST)[i * HD : (i + 1) * HD])
+            dk.append(matmul(dsb, q))
+            dv.append(matmul(pr.astype(BF16), do))
+        G[rr, qc] = jnp.transpose(jnp.concatenate(dq, axis=0)).astype(BF16)
+        G[rr, kc] = jnp.where(lane == 0, dk[0], dk[1]).astype(BF16)
+        G[rr, vc] = jnp.where(lane == 0, dv[0], dv[1]).astype(BF16)
+
+    for hp in range(half_heads // 2):
+        attend_back(c, hp)
+        if hp == 0:
+            gmcp.wait()
+
+            def add_pair(i, _):
+                for j in range(Y * X):
+                    add_into(GM, (i, j // X, j % X, slice(None), span(c * HW, HW)), r["GMR"].at[i, j // X, j % X])
+                return 0
+
+            lax.fori_loop(0, Z, add_pair, 0)
+            first_pair("m")
+            events[:0] = (rs_events("x") + rs_events("m"))[::-1]
+        pump(1)
+    docp.wait()
+    for hp in range(half_heads // 2):
+        attend_back(o, hp)
+        pump(1)
+
+    for t in range(Z):
+        g = contract(N1[:, t * DT : (t + 1) * DT], G[:, 0 : 3 * HW], FIRST)
+        GJ[t, :, :, :, 0 : 3 * HW] = g.astype(BF16).reshape(Y, X, rows["j"], 3 * HW)
+    first_pair("j")
+    events[:0] = rs_events("j")[::-1]
+    gather_done("j")
+    for t in range(3):
+        VG[6 + t * HW // D : 7 + t * HW // D, t * HW % D : t * HW % D + HW] += jnp.sum(
+            G[:, t * HW : (t + 1) * HW].astype(F32), axis=0, keepdims=True
+        )
+
+    back_part(G, W["j"], 3 * HW, sib)
+    dn1cp = to_pair(XS, XR)
+    pump(2)
+    dn1cp.wait()
+    for t in range(R // TR):
+        rr = pl.ds(t * TR, TR)
+        dy = contract(G[span(c * R + t * TR, TR), 0 : 3 * HW], W["j"][...].reshape(D, 3 * HW), LAST) + XR[rr, :].astype(F32)
+        scaled, inverse = normed(h0[rr, :])
+        H1[rr, :] = H1[rr, :] + norm_back(dy, scaled, inverse, V[0:1, :], 0)
+    gtcp = pltpu.make_async_copy(H1, r["gt"], r["fl"].at[len(gorder) + 1])
+    gtcp.start()
+
+    VGR = r["VGR"]
+    for slot, to in ((0, to_x), (1, to_y)):
+        cp = remote(VG, VGR.at[slot], r["gs"].at[slot], r["gr"].at[slot], to)
+        cp.start()
+        cp.wait()
+        VG[...] = VG[...] + VGR[slot]
+        pump(1)
+    cps = []
+    for d in range(1, Z):
+        cp = remote(VG, VGR.at[1 + d], r["gs"].at[1 + d], r["gr"].at[1 + d], to_z[d])
+        cp.start()
+        cps.append(cp)
+    for cp in cps:
+        cp.wait()
+    acc = VG[...]
+    for d in range(1, Z):
+        acc = acc + VGR[1 + d]
+    ov = r["ov"]
+    ov[c] = acc
+    cp = to_pair(ov.at[c], ov.at[c])
+
+    pump(len(events))
+    cp.wait()
+    for k in gorder:
+        for p in (0, 1):
+            rs_first(k, p).wait_send()
+            rs_second(k, p).wait_send()
+            for d in range(1, Z):
+                rs_third(k, p, d).wait_send()
+    for f in fin_copies:
+        f.wait()
+    outcp.wait()
+    gtcp.wait()
+
+
+def spread_vector(piece, me, count):
+    n = piece.shape[0]
+    place = jnp.arange(n * count, dtype=jnp.int32) // n
+    return jnp.where(place == me, jnp.tile(piece, count), 0).astype(BF16)
+
+
+def fused_layer(dims, *args):
+    (
+        tokens,
+        kept_patch,
+        image_lengths,
+        ground_distance,
+        cotangent,
+        norm_one_gain,
+        norm_one_bias,
+        joint_weight,
+        joint_bias,
+        merge_weight,
+        merge_bias,
+        norm_two_gain,
+        norm_two_bias,
+        expand_weight,
+        expand_bias,
+        shrink_weight,
+        shrink_bias,
+    ) = args
+    Z, Y, X = dims
+    N = Z * Y * X
+    R, D = tokens.shape
+    FF = expand_weight.shape[1]
+    HW, FC, blk = D // 2, FF // 2, shrink_weight.shape[0] // 2
+    rj = joint_weight.shape[0]
+    me, c = lax.axis_index("dp"), lax.axis_index("rep")
+    segment, live = packing(image_lengths[0], R)
+    ground_rows = row_distance(segment, ground_distance[0])
+    h0 = tokens.astype(F32) + positions(kept_patch, ground_rows, D)
+    seg = jnp.broadcast_to(segment.astype(F32)[None, :], (8, R))
+    jb = spread_vector(joint_bias, me, N).reshape(3, 2, HW)
+    jb = jnp.where(c == 0, jb[:, 0], jb[:, 1]).reshape(-1)
+    xb = spread_vector(expand_bias, me, N).reshape(FF // (2 * blk), 2, blk)
+    xb = jnp.where(c == 0, xb[:, 0], xb[:, 1]).reshape(-1)
+    flat = [
+        spread_vector(v, me, N)
+        for v in (norm_one_gain, norm_one_bias, merge_bias, norm_two_gain, norm_two_bias, shrink_bias)
+    ]
+    flat += [jb, jnp.zeros((2 * D - 3 * HW,), BF16), xb]
+    vec = jnp.concatenate(flat).reshape(-1, D)
+    vec = jnp.pad(vec, ((0, 16 - vec.shape[0]), (0, 0)))
+
+    vm, hbm = pl.BlockSpec(memory_space=pltpu.VMEM), pl.BlockSpec(memory_space=pl.ANY)
+    ins = [("h0", h0, vm), ("live", live[:, None], vm), ("seg", seg, vm), ("vec", vec, vm), ("cot", cotangent, hbm)]
+    ins += [("wj", joint_weight, hbm), ("wm", merge_weight, hbm), ("wx", expand_weight, hbm), ("ws", shrink_weight, hbm)]
+    S = jax.ShapeDtypeStruct
+    outs = [
+        ("out", S((R, D), BF16), hbm),
+        ("gt", S((R, D), F32), hbm),
+        ("oj", S((2, rj, 3 * HW), BF16), hbm),
+        ("om", S((2, rj, HW), BF16), hbm),
+        ("ox", S((2, 2 * rj, FC // 2), BF16), hbm),
+        ("os", S((2, blk, D), BF16), hbm),
+        ("ov", S((2, 16, D), F32), vm),
+    ]
+    V = pltpu.VMEM
+    dma = pltpu.SemaphoreType.DMA
+    cut = {"j": (rj, 3 * HW // 2), "m": (rj, HW // 2), "x": (rj, FC // 2), "s": (blk, D // 2)}
+    scratch = [
+        ("Wj", V((Z, Y, X, rj, 3 * HW), BF16)),
+        ("Wm", V((Z, Y, X, rj, D), BF16)),
+        ("Wx", V((Z, Y, X, rj, FC), BF16)),
+        ("Ws", V((Z, Y, X, blk, D), BF16)),
+        ("GS", V((Z, Y, X, blk, D), BF16)),
+        ("GM", V((Z, Y, X, rj, D), BF16)),
+        ("GMR", V((Z, Y, X, rj, HW), BF16)),
+        ("N1", V((2 * R, D), BF16)),
+        ("QKV", V((2 * R, 3 * HW), BF16)),
+        ("OA", V((R, D), BF16)),
+        ("H1", V((R, D), F32)),
+        ("N2", V((2 * R, D), BF16)),
+        ("G", V((2 * R, FC), BF16)),
+        ("DU", V((2 * R, FC), BF16)),
+        ("EB", V((2 * R, D), BF16)),
+        ("SEG", V((2, 8, R), F32)),
+        ("L", V((D // HD, 1, R), F32)),
+        ("V", V((16, D), F32)),
+        ("VR", V((Z + 1, 16, D), BF16)),
+        ("VT", V((2, 16, D), BF16)),
+        ("VG", V((16, D), F32)),
+        ("VGR", V((Z + 1, 16, D), F32)),
+        ("XS", V((R, D), BF16)),
+        ("XR", V((R, D), BF16)),
+        ("OUTB", V((R, D), BF16)),
+        ("DA", V((R, D), BF16)),
+    ]
+    for k, (a, b) in cut.items():
+        scratch += [("R1" + k, V((2, Z, 2, a, b), BF16)), ("R2" + k, V((2, Z, a, b), BF16))]
+        scratch += [("R3" + k, V((2, Z - 1, a, b), BF16))]
+    scratch += [
+        ("ps", dma((12,))),
+        ("pr", dma((12,))),
+        ("vs", dma((Z + 1,))),
+        ("vr", dma((Z + 1,))),
+        ("gs", dma((Z + 1,))),
+        ("gr", dma((Z + 1,))),
+        ("ls", dma((5,))),
+        ("as1", dma((8,))),
+        ("ar1", dma((8, Z - 1))),
+        ("as2", dma((8,))),
+        ("ar2", dma((8, Z))),
+        ("as3", dma((8,))),
+        ("ar3", dma((8,))),
+        ("rs1", dma((8,))),
+        ("rr1", dma((8,))),
+        ("rs2", dma((8,))),
+        ("rr2", dma((8,))),
+        ("rs3", dma((8, Z - 1))),
+        ("rr3", dma((8, Z - 1))),
+        ("fl", dma((6,))),
+        ("fs", dma((4,))),
+        ("fr", dma((4,))),
+    ]
+    names = [n for n, *_ in ins + outs + scratch]
+    res = pl.pallas_call(
+        functools.partial(layer_kernel, dims, names),
+        out_shape=[s for _, s, _ in outs],
+        in_specs=[s for _, _, s in ins],
+        out_specs=[s for _, _, s in outs],
+        scratch_shapes=[s for _, s in scratch],
+        compiler_params=pltpu.CompilerParams(
+            collective_id=0, has_side_effects=True, vmem_limit_bytes=VMEM_BYTES
+        ),
+    )(*[a for _, a, _ in ins])
+    out, gt, oj, om, ox, os_, ov = res
+    g_joint = oj.reshape(2, rj, 3, HW).transpose(1, 2, 0, 3).reshape(rj, 3 * D).astype(F32)
+    g_merge = om.transpose(1, 0, 2).reshape(rj, D).astype(F32)
+    g_expand = (
+        ox.reshape(2, 2, rj, FC // (2 * blk), blk).transpose(2, 1, 3, 0, 4).reshape(rj, FF).astype(F32)
+    )
+    g_shrink = os_.reshape(2 * blk, D).astype(F32)
+    both = ov[0, 0:6] + ov[1, 0:6]
+
+    def mine(v):
+        return lax.dynamic_slice_in_dim(v, me * (v.shape[0] // N), v.shape[0] // N)
+
+    g_jb = mine(ov[:, 6:8].reshape(2, 2 * D)[:, : 3 * HW].reshape(2, 3, HW).transpose(1, 0, 2).reshape(-1))
+    g_xb = mine(ov[:, 8:10].reshape(2, FC // blk, blk).transpose(1, 0, 2).reshape(-1))
+    g1, b1, mb, g2, b2, sb = (mine(both[i]) for i in range(6))
+    return out, gt, g1, b1, g_joint, g_jb, g_merge, mb, g2, b2, g_expand, g_xb, g_shrink, sb
+
+
+def layout(mesh, joint_rows, shrink_rows):
+    n = mesh.shape["dp"]
+    if mesh.shape["rep"] != 2 or n % 8 or joint_rows % 16 or shrink_rows % 256:
+        return None
+    return (n // 4, 2, 2)
+
+
+def on_device(mesh, *args):
+    dims = layout(mesh, args[7].shape[0], args[15].shape[0])
+    if dims is None:
+        return general_layer(*args)
+    return fused_layer(dims, *args)
+
+
 def solution(mesh):
+    rows, rows2 = P(("dp", "rep")), P(("dp", "rep"), None)
+    vector, matrix = P("dp"), P("dp", None)
     return jax.shard_map(
-        on_device,
+        functools.partial(on_device, mesh),
         mesh=mesh,
         in_specs=(
-            P(("dp", "rep"), None),
-            P(("dp", "rep")),
-            P(("dp", "rep"), None),
-            P(("dp", "rep"), None),
-            P(("dp", "rep"), None),
-            P("dp"),
-            P("dp"),
-            P("dp", None),
-            P("dp"),
-            P("dp", None),
-            P("dp"),
-            P("dp"),
-            P("dp"),
-            P("dp", None),
-            P("dp"),
-            P("dp", None),
-            P("dp"),
+            rows2,
+            rows,
+            rows2,
+            rows2,
+            rows2,
+            vector,
+            vector,
+            matrix,
+            vector,
+            matrix,
+            vector,
+            vector,
+            vector,
+            matrix,
+            vector,
+            matrix,
+            vector,
         ),
         out_specs=(
-            P(("dp", "rep"), None),
-            P(("dp", "rep"), None),
-            P("dp"),
-            P("dp"),
-            P("dp", None),
-            P("dp"),
-            P("dp", None),
-            P("dp"),
-            P("dp"),
-            P("dp"),
-            P("dp", None),
-            P("dp"),
-            P("dp", None),
-            P("dp"),
+            rows2,
+            rows2,
+            vector,
+            vector,
+            matrix,
+            vector,
+            matrix,
+            vector,
+            vector,
+            vector,
+            matrix,
+            vector,
+            matrix,
+            vector,
         ),
         check_vma=False,
     )

time: 1480 us -> 330 us (0.22)
  waiting for transfers between devices: 993 us -> 0 us
  Pallas kernels: 0 us -> 294 us
  matrix products: 200 us -> 0 us
  blocking collectives: 195 us -> 0 us
  other arithmetic: 44.3 us -> 11.6 us
  between operations: 18 us -> 1.43 us
    reduce_scatter x4 -> x0, waiting for transfers between devices: 791 us -> none  [the longest x1 352 us: on_device(): lax.psum_scatter(grads_full[10], 'dp', scatter_dimension=0, tiled=True)]
    pallas_call x0 -> x1, Pallas kernels: none -> 294 us  [fused_layer(): pl.pallas_call(functools.partial(layer_kernel, dims, names), out_shape=[s...]
    dot_general x18 -> x0, matrix products: 200 us -> none  [the longest x1 27.7 us: on_device(): jnp.dot(second_low, full[8], preferred_element_type=jnp.float32)]
    all_gather x4 -> x0, waiting for transfers between devices: 182 us -> none  [the longest x1 96.4 us: on_device(): lax.all_gather(expand_weight, 'dp', axis=0, tiled=True)]
    unnamed x2 -> x0, blocking collectives: 157 us -> none
    all_gather x1 -> x0, blocking collectives: 35.5 us -> none  [on_device(): lax.all_gather(expand_bias, 'dp', axis=0, tiled=True)]
    convert_element_type x24 -> x2, other arithmetic: 19.9 us -> 2.13 us  [the longest x1 2.13 us: fused_layer(): g_shrink = os_.reshape(2 * blk, D).astype(F32)]
    psum x1 -> x0, waiting for transfers between devices: 17.7 us -> none  [on_device(): lax.psum(shares[2].astype(jnp.bfloat16), 'rep').astype(jnp.float32)]
  transfers between devices with their start and end apart: 9 -> 0, of which waited for: 6 -> 0; matrix products, arithmetic and copies ran while one was open for 16% -> 0% of each run, Pallas kernels for 0% -> 0%
where the time goes in v1:
time: 330 us; the launch traced here: 324 us
  Pallas kernels  294 us (89%)
  local copies, waits for them, and re-layouts  17.6 us (5%)
  other arithmetic  11.6 us (4%)
    pallas_call x1, Pallas kernels, fused_layer(): pl.pallas_call(functools.partial(layer_kernel, dims, names), out_shape=[s...  294 us

profile of v1, /device:TPU:0, one launch (start us, length us, event | category | flops | bytes accessed | tf_op | source)
XLA Modules:
  0.0 324.3 jit_solution(11326505321156530883)
XLA Ops:
  0.7 0.7 convert_bitcast_fusion.1
  1.4 0.7 copy.45
  2.2 0.1 reduce
  2.3 0.1 convert_reduce_fusion
  2.4 0.1 select_reduce_fusion
  2.5 0.7 convert_multiply_fusion
  3.2 3.7 %multiply_sine_fusion.1 = (f32[512,256]{1,0:T(8,128)S(1)}, f32[512,256]{1,0:T(8,128)S(1)}, f32[512,256]{1,0:T(8,128)S(1)}, f32[512,256]{1,0:T(8,128)S(1)}) fusion(f32[256]{0:T(256)S(1)} %negate_power_fusion, f32[512]{0:T(512)S(1)} %get-tuple-element.36, f32[512]{0:T(512)S(1)} %get-tuple-element.37), kind=kLoop, calls=%fused_computation.4 | loop fusion | flops 262144 | bytes 2102272 | tf_op jit(solution)/shard_map/sin | solution.py:40
  7.0 1.6 maximum_add_fusion.args_0_
  8.6 0.5 slice.71
  9.2 1.4 fusion.args_1_
  10.5 0.6 broadcast_in_dim.35.args_2_
  12.0 0.3 dynamic-update-slice.6
  12.3 0.2 dynamic-update-slice.7
  12.6 0.6 pad.4.args_3_
  13.2 293.6 %shard_map.272 = (bf16[512,1024]{1,0:T(8,128)(2,1)}, f32[512,1024]{1,0:T(8,128)}, bf16[2,64,1536]{2,1,0:T(8,128)(2,1)}, bf16[2,64,512]{2,1,0:T(8,128)(2,1)}, bf1...) custom-call(f32[512,1024]{1,0:T(8,128)} %maximum_add_fusion.args_0_, ...), custom_call_target="tpu_custom_call" | custom-call | tf_op jit(solution)/shard_map/pallas_call | solution.py:980
  306.8 0.8 slice_add_fusion
  307.6 0.6 fusion.16
  308.2 2.0 reshape.168
  310.2 0.6 copy.46
  310.8 1.6 reshape.164
  312.4 0.9 fusion.22
  313.3 0.6 dynamic_slice.40
  314.0 0.7 copy.51
  314.7 0.6 fusion.18
  315.3 0.6 fusion.20
  315.9 0.1 copy.54
  316.0 0.8 copy.49
  316.9 1.8 reshape.166
  318.7 0.6 dynamic_slice.47
  319.4 2.1 bitcast_convert_fusion
  321.5 1.0 copy.67
  322.5 1.3 copy.68
  (65 shorter events, 1.1 us)
Async XLA Ops:
  0.6 6.3 %copy-start.1 = (bf16[512,1024]{1,0:T(8,128)(2,1)S(1)}, bf16[512,1024]{1,0:T(8,128)(2,1)}, u32[]{:S(2)}) copy-start(bf16[512,1024]{1,0:T(8,128)(2,1)} %param.17) | copy-start | bytes 3145732
  6.9 4.2 %copy-start.5 = (bf16[64]{0:T(256)(128)(2,1)S(1)}, bf16[64]{0:T(256)(128)(2,1)}, u32[]{:S(2)}) copy-start(bf16[64]{0:T(256)(128)(2,1)} %param.22) | copy-start | bytes 388
  6.9 4.3 %copy-start.6 = (bf16[64]{0:T(256)(128)(2,1)S(1)}, bf16[64]{0:T(256)(128)(2,1)}, u32[]{:S(2)}) copy-start(bf16[64]{0:T(256)(128)(2,1)} %param.23) | copy-start | bytes 388
  6.9 4.4 %copy-start.7 = (bf16[64]{0:T(256)(128)(2,1)S(1)}, bf16[64]{0:T(256)(128)(2,1)}, u32[]{:S(2)}) copy-start(bf16[64]{0:T(256)(128)(2,1)} %param.27) | copy-start | bytes 388
  6.9 4.5 %copy-start.8 = (bf16[64]{0:T(256)(128)(2,1)S(1)}, bf16[64]{0:T(256)(128)(2,1)}, u32[]{:S(2)}) copy-start(bf16[64]{0:T(256)(128)(2,1)} %param.28) | copy-start | bytes 388
  7.0 4.6 %copy-start.9 = (bf16[64]{0:T(256)(128)(2,1)S(1)}, bf16[64]{0:T(256)(128)(2,1)}, u32[]{:S(2)}) copy-start(bf16[64]{0:T(256)(128)(2,1)} %param.29) | copy-start | bytes 388
  7.0 4.7 %copy-start.10 = (bf16[64]{0:T(256)(128)(2,1)S(1)}, bf16[64]{0:T(256)(128)(2,1)}, u32[]{:S(2)}) copy-start(bf16[64]{0:T(256)(128)(2,1)} %param.33) | copy-start | bytes 388
  7.0 4.8 %copy-start.11 = (bf16[192]{0:T(256)(128)(2,1)S(1)}, bf16[192]{0:T(256)(128)(2,1)}, u32[]{:S(2)}) copy-start(bf16[192]{0:T(256)(128)(2,1)} %param.25) | copy-start | bytes 1156
  7.0 5.5 %copy-start.12 = (bf16[256]{0:T(256)(128)(2,1)S(1)}, bf16[256]{0:T(256)(128)(2,1)}, u32[]{:S(2)}) copy-start(bf16[256]{0:T(256)(128)(2,1)} %param.31) | copy-start | bytes 1540
  310.2 3.8 %copy-start.4 = (bf16[2,64,512]{2,1,0:T(8,128)(2,1)S(1)}, bf16[2,64,512]{2,1,0:T(8,128)(2,1)}, u32[]{:S(2)}) copy-start(bf16[2,64,512]{2,1,0:T(8,128)(2,1)} %get-tuple-element.25) | copy-start | bytes 393220
  310.2 5.7 %copy-start.3 = (bf16[2,128,1024]{2,1,0:T(8,128)(2,1)S(1)}, bf16[2,128,1024]{2,1,0:T(8,128)(2,1)}, u32[]{:S(2)}) copy-start(bf16[2,128,1024]{2,1,0:T(8,128)(2,1)} %get-tuple-element.26) | copy-start | bytes 1572868
  316.9 4.6 %copy-start.2 = (bf16[512,1024]{1,0:T(8,128)(2,1)S(1)}, bf16[512,1024]{1,0:T(8,128)(2,1)}, u32[]{:S(2)}) copy-start(bf16[512,1024]{1,0:T(8,128)(2,1)} %get-tuple-element.64) | copy-start | bytes 3145732
  318.7 3.8 %copy-start = (f32[512,1024]{1,0:T(8,128)S(1)}, f32[512,1024]{1,0:T(8,128)}, u32[]{:S(2)}) copy-start(f32[512,1024]{1,0:T(8,128)} %get-tuple-element.65) | copy-start | bytes 6291460
